TPU v7x, 32 devices: a whole 2x2x4 slice. The times are simulated.
32 devices in a mesh: ctx: 16 (over z, y, x), head: 2 (over core).
Axes of the slice: x: 2, y: 2, z: 4, core: 2. Of those that a mesh axis runs over, the one named last changes fastest.
Arguments:
- queries: bfloat16 [4096, 4096], P('ctx', 'head'), may hold values from -6.5 to 6.5
- keyval: bfloat16 [2, 4096, 1024], P(None, 'ctx', 'head'), may hold values from -6 to 6
- out_gain: float32 [4096], P('head'), may hold values from 0.1 to 1.9
Outputs:
- attended: bfloat16 [4096, 4096], P('ctx', 'head')
All inputs are finite; a program needn't handle non-finite values.
Results may differ from a plain program's by a relative error of at most 0.0049.
Values may be sent and summed in bfloat16 or wider, within the bound.
A program may use at most 64 MiB of HBM per device.

v0:
```python
import jax
import jax.numpy as jnp
import numpy as np
from jax import lax
from jax.sharding import PartitionSpec as P

HEADS = 32
HD = 128
BLK = 128


def shifted(value, axis, steps):
    count = lax.axis_size(axis)
    first, last = (max(0, -steps), min(count, count - steps))
    return lax.ppermute(value, axis, [(source, source + steps) for source in range(first, last)])


def local(queries, keyval, out_gain):
    tok_rows = queries.shape[0]
    blocks = tok_rows // BLK
    kv_local = keyval.shape[2] // HD
    group_size = queries.shape[1] // HD // kv_local
    ctx_count = lax.axis_size("ctx")
    levels = ctx_count.bit_length() - 1
    position = lax.axis_index("ctx")
    panels = []
    for power_level in range(levels):
        panels.append(shifted(keyval, "ctx", 2**power_level))
    near_dist = [0] + [2**0]
    extended = jnp.concatenate([panels[0], keyval], axis=1).reshape(
        2, 2 * blocks, BLK, kv_local, HD
    )
    near_table = np.array(
        [[block_row + blocks - gap_size for gap_size in near_dist] for block_row in range(blocks)],
        np.int32,
    )
    near_keys = extended[:, near_table]
    far_keys = jnp.stack([panel.reshape(2, blocks, BLK, kv_local, HD) for panel in panels], axis=2)
    selected = jnp.concatenate([near_keys, far_keys], axis=2)
    slots = selected.shape[2]
    block_ids = position * blocks + jnp.arange(blocks, dtype=jnp.int32)
    near_valid = block_ids[:, None] - jnp.array(near_dist, jnp.int32)[None, :] >= 0
    far_reach = jnp.array([2**power_level for power_level in range(levels)], jnp.int32)
    far_valid = jnp.broadcast_to((position >= far_reach)[None, :], (blocks, levels))
    valid_slot = jnp.concatenate([near_valid, far_valid], axis=1)
    lower_tri = jnp.arange(BLK)[:, None] >= jnp.arange(BLK)[None, :]
    own_slot = jnp.arange(slots) == 0
    allowed = valid_slot[:, :, None, None] & (own_slot[None, :, None, None] | lower_tri[None, None])
    score_mask = allowed.transpose(0, 2, 1, 3)[:, None]
    score_scale = HD ** (-0.5)
    grouped = queries.reshape(blocks, BLK, kv_local, group_size, HD).transpose(2, 0, 3, 1, 4)
    key_heads = selected[0].transpose(3, 0, 1, 2, 4)
    value_heads = selected[1].transpose(3, 0, 1, 2, 4)

    def attend_head(operands):
        query_head, key_head, value_head = operands
        scores = (
            jnp.einsum("bgqd,bskd->bgqsk", query_head, key_head, preferred_element_type=jnp.float32)
            * score_scale
        )
        scores = jnp.where(score_mask, scores, -jnp.inf)
        row_max = jnp.max(scores, axis=(3, 4), keepdims=True)
        weights = jnp.exp(scores - row_max)
        row_sum = jnp.sum(weights, axis=(3, 4), keepdims=True)
        probabilities = (weights / row_sum).astype(jnp.bfloat16)
        return jnp.einsum(
            "bgqsk,bskd->bgqd", probabilities, value_head, preferred_element_type=jnp.float32
        )

    head_outs = lax.map(attend_head, (grouped, key_heads, value_heads))
    combined = head_outs.transpose(1, 3, 0, 2, 4).reshape(tok_rows, kv_local * group_size * HD)
    squares = jnp.sum(combined * combined, axis=1)
    square_sum = lax.psum(squares, "head")
    inverse = lax.rsqrt(square_sum / (HEADS * HD) + 1e-06)
    return (combined * inverse[:, None] * out_gain[None, :]).astype(jnp.bfloat16)


def solution(mesh):
    in_specs = (P("ctx", "head"), P(None, "ctx", "head"), P("head"))
    out_specs = P("ctx", "head")
    return jax.shard_map(local, mesh=mesh, in_specs=in_specs, out_specs=out_specs, check_vma=False)
```

profile of v0, /device:TPU:31, one launch (start us, length us, event | category | flops | bytes accessed | tf_op | source)
XLA Modules:
  0.0 101.4 jit_solution(1402346842485954238)
XLA Ops:
  0.0 1.3 %collective-permute-start = (bf16[2,256,512]{2,1,0:T(8,128)(2,1)}, bf16[2,256,512]{2,1,0:T(8,128)(2,1)}, u32[]{:S(2)}, u32[]{:S(2)}) collective-permute-start(bf16[2,256,512]{2,1,0:T(8,128)(2,1)} %param.10), channel_id=1, source_target_pairs={{0,2},{2,4},{4,6},{6,8},{8,10},{10,12},{12,14},{14,16},{16,18},{18... | collective-permute-start | bytes 1572872 | tf_op jit(solution)/shard_map/ppermute | solution.py:15
  1.3 1.3 %collective-permute-start.1 = (bf16[2,256,512]{2,1,0:T(8,128)(2,1)}, bf16[2,256,512]{2,1,0:T(8,128)(2,1)}, u32[]{:S(2)}, u32[]{:S(2)}) collective-permute-start(bf16[2,256,512]{2,1,0:T(8,128)(2,1)} %param.10), channel_id=1, source_target_pairs={{0,4},{2,6},{4,8},{6,10},{8,12},{10,14},{12,16},{14,18},{16,20},{1... | collective-permute-start | bytes 1572872 | tf_op jit(solution)/shard_map/ppermute | solution.py:15
  2.6 1.3 %collective-permute-start.2 = (bf16[2,256,512]{2,1,0:T(8,128)(2,1)}, bf16[2,256,512]{2,1,0:T(8,128)(2,1)}, u32[]{:S(2)}, u32[]{:S(2)}) collective-permute-start(bf16[2,256,512]{2,1,0:T(8,128)(2,1)} %param.10), channel_id=1, source_target_pairs={{0,8},{2,10},{4,12},{6,14},{8,16},{10,18},{12,20},{14,22},{16,24},... | collective-permute-start | bytes 1572872 | tf_op jit(solution)/shard_map/ppermute | solution.py:15
  3.9 1.3 %collective-permute-start.3 = (bf16[2,256,512]{2,1,0:T(8,128)(2,1)}, bf16[2,256,512]{2,1,0:T(8,128)(2,1)}, u32[]{:S(2)}, u32[]{:S(2)}) collective-permute-start(bf16[2,256,512]{2,1,0:T(8,128)(2,1)} %param.10), channel_id=1, source_target_pairs={{0,16},{2,18},{4,20},{6,22},{8,24},{10,26},{12,28},{14,30},{1,17},... | collective-permute-start | bytes 1572872 | tf_op jit(solution)/shard_map/ppermute | solution.py:15
  5.2 0.7 pad_clamp_fusion
  5.9 0.1 fusion.16
  6.0 0.7 broadcast_compare_fusion
  6.6 1.8 %reshape.49 = bf16[2,128,4,4,128]{4,3,2,1,0:T(4,128)(2,1)S(1)} reshape(bf16[256,2048]{1,0:T(8,128)(2,1)} %param.9) | data formatting | bytes 2097152 | tf_op jit(solution)/shard_map/reshape | solution.py:51
  8.4 0.1 pad.1.clone
  8.5 0.1 broadcast_or_fusion
  8.6 6.4 %collective-permute-done = bf16[2,256,512]{2,1,0:T(8,128)(2,1)} collective-permute-done((bf16[2,256,512]{2,1,0:T(8,128)(2,1)}, bf16[2,256,512]{2,1,0:T(8,128)(2,1)}, u32[]{:S(2)}, u32[]{:S(2)}) %collective-permute-start) | collective-permute-done | bytes 524320 | tf_op jit(solution)/shard_map/ppermute | solution.py:15
  15.0 2.2 %pad_maximum_fusion = bf16[2,512,512]{2,1,0:T(8,128)(2,1)} fusion(bf16[2,256,512]{2,1,0:T(8,128)(2,1)} %param.10, bf16[2,256,512]{2,1,0:T(8,128)(2,1)} %collective-permute-done), kind=kLoop, calls=%fused_computation.26 | loop fusion | flops 2097152 | bytes 2097152 | tf_op jit(solution)/shard_map/concatenate | solution.py:30
  17.2 2.2 %reshape.50 = bf16[2,4,128,4,128]{4,3,2,1,0:T(4,128)(2,1)} reshape(bf16[2,512,512]{2,1,0:T(8,128)(2,1)} %pad_maximum_fusion) | data formatting | bytes 2097152 | tf_op jit(solution)/shard_map/reshape | solution.py:30
  19.4 2.5 %copy.19 = bf16[2,4,128,4,128]{4,2,3,1,0:T(8,128)(2,1)} copy(bf16[2,4,128,4,128]{4,3,2,1,0:T(4,128)(2,1)} %reshape.50) | data formatting | bytes 2097152 | tf_op jit(solution)/shard_map/reshape | solution.py:30
  21.8 2.9 %gather_fusion = bf16[4,2,128,4,128]{4,2,3,1,0:T(8,128)(2,1)} fusion(bf16[2,4,128,4,128]{4,2,3,1,0:T(8,128)(2,1)} %copy.19, s32[1024]{0:T(1024)S(1)} %pad_clamp_fusion), kind=kCustom, calls=%fused_computation | custom fusion | bytes 2097168 | tf_op jit(solution)/shard_map/gather | solution.py:37
  24.7 2.0 %stack_reshape.12 = bf16[2,2,1,128,4,128]{5,4,3,1,0,2:T(4,128)(2,1)} reshape(bf16[2,256,512]{2,1,0:T(8,128)(2,1)} %collective-permute-done) | data formatting | bytes 1048576 | tf_op jit(solution)/shard_map/stack;reshape | solution.py:38
  26.7 2.5 %bitcast_dynamic-update-slice_fusion = bf16[2,2,6,128,4,128]{5,3,2,1,4,0:T(8,128)(2,1)} fusion(bf16[2,2,2,128,4,128]{5,3,4,2,1,0:T(8,128)(2,1)} %bitcast.57), kind=kLoop, calls=%fused_computation.27 | loop fusion | bytes 2097152
  29.2 1.9 %copy_dynamic-update-slice_fusion.3 = bf16[2,2,6,128,4,128]{5,3,2,1,4,0:T(8,128)(2,1)} fusion(bf16[2,2,6,128,4,128]{5,3,2,1,4,0:T(8,128)(2,1)} %bitcast_dynamic-update-slice_fusion, bf16[2,2,1,128,4,128]{5,4,3,1,0,2:T(4,128)(2,1)} %stack_reshape.12), kind=kLoop, calls=%fused_computation.31 | loop fusion | bytes 1048576
  31.2 0.0 collective-permute-done.1
  31.2 2.0 %stack_reshape.13 = bf16[2,2,1,128,4,128]{5,4,3,1,0,2:T(4,128)(2,1)} reshape(bf16[2,256,512]{2,1,0:T(8,128)(2,1)} %collective-permute-done.1) | data formatting | bytes 1048576 | tf_op jit(solution)/shard_map/stack;reshape | solution.py:38
  33.1 9.1 %collective-permute-done.2 = bf16[2,256,512]{2,1,0:T(8,128)(2,1)} collective-permute-done((bf16[2,256,512]{2,1,0:T(8,128)(2,1)}, bf16[2,256,512]{2,1,0:T(8,128)(2,1)}, u32[]{:S(2)}, u32[]{:S(2)}) %collective-permute-start.2) | collective-permute-done | bytes 524320 | tf_op jit(solution)/shard_map/ppermute | solution.py:15
  42.2 2.0 %stack_reshape.14 = bf16[2,2,1,128,4,128]{5,4,3,1,0,2:T(4,128)(2,1)} reshape(bf16[2,256,512]{2,1,0:T(8,128)(2,1)} %collective-permute-done.2) | data formatting | bytes 1048576 | tf_op jit(solution)/shard_map/stack;reshape | solution.py:38
  44.2 2.0 %copy_dynamic-update-slice_fusion.2 = bf16[2,2,6,128,4,128]{5,3,2,1,4,0:T(8,128)(2,1)} fusion(bf16[2,2,6,128,4,128]{5,3,2,1,4,0:T(8,128)(2,1)} %copy_dynamic-update-slice_fusion.3, bf16[2,2,1,128,4,128]{5,4,3,1,0,2:T(4,128)(2,1)} %stack_reshape.13), kind=kLoop, calls=%fused_computation.30 | loop fusion | bytes 1048576
  46.1 1.9 %copy_dynamic-update-slice_fusion.1 = bf16[2,2,6,128,4,128]{5,3,2,1,4,0:T(8,128)(2,1)} fusion(bf16[2,2,6,128,4,128]{5,3,2,1,4,0:T(8,128)(2,1)} %copy_dynamic-update-slice_fusion.2, bf16[2,2,1,128,4,128]{5,4,3,1,0,2:T(4,128)(2,1)} %stack_reshape.14), kind=kLoop, calls=%fused_computation.29 | loop fusion | bytes 1048576
  48.1 16.5 %collective-permute-done.3 = bf16[2,256,512]{2,1,0:T(8,128)(2,1)} collective-permute-done((bf16[2,256,512]{2,1,0:T(8,128)(2,1)}, bf16[2,256,512]{2,1,0:T(8,128)(2,1)}, u32[]{:S(2)}, u32[]{:S(2)}) %collective-permute-start.3) | collective-permute-done | bytes 524320 | tf_op jit(solution)/shard_map/ppermute | solution.py:15
  64.6 2.0 %stack_reshape.15 = bf16[2,2,1,128,4,128]{5,4,3,1,0,2:T(4,128)(2,1)} reshape(bf16[2,256,512]{2,1,0:T(8,128)(2,1)} %collective-permute-done.3) | data formatting | bytes 1048576 | tf_op jit(solution)/shard_map/stack;reshape | solution.py:38
  66.5 1.9 %copy_dynamic-update-slice_fusion = bf16[2,2,6,128,4,128]{5,3,2,1,4,0:T(8,128)(2,1)} fusion(bf16[2,2,6,128,4,128]{5,3,2,1,4,0:T(8,128)(2,1)} %copy_dynamic-update-slice_fusion.1, bf16[2,2,1,128,4,128]{5,4,3,1,0,2:T(4,128)(2,1)} %stack_reshape.15), kind=kLoop, calls=%fused_computation.28 | loop fusion | bytes 1048576 | tf_op jit(solution)/shard_map/concatenate | solution.py:39
  68.5 4.0 %slice_bitcast_fusion = (bf16[4,2,6,128,128]{4,3,2,1,0:T(8,128)(2,1)}, bf16[4,2,6,128,128]{4,3,2,1,0:T(8,128)(2,1)}) fusion(bf16[2,2,6,128,4,128]{5,3,2,1,4,0:T(8,128)(2,1)} %copy_dynamic-update-slice_fusion), kind=kLoop, calls=%fused_computation.24 | loop fusion | bytes 6291456 | tf_op jit(solution)/shard_map/transpose | solution.py:53
  72.5 18.9 %while.11 = (s32[]{:T(128)}, f32[4,2,4,128,128]{4,3,2,1,0:T(8,128)S(1)}, bf16[4,2,4,128,128]{4,2,0,3,1:T(4,128)(2,1)S(1)}, bf16[4,2,6,128,128]{4,3,2,1,0:T(8,128...) while((s32[]{:T(128)}, ...), condition=%wide.region_3.4_spmd.clone, body=%wide.region_0.3_spmd.clone.sunk | while | flops 412284928 | bytes 12441189 | solution.py:70
  72.5 0.1 constant_dynamic-slice_fusion.2
  72.6 0.2 and_bitcast_fusion.2
  72.7 1.6 %fusion.22 = (f32[2,4,128]{2,1,0:T(4,128)S(1)}, f32[2,4,128,6,128]{2,4,3,1,0:T(8,128)S(1)}) fusion(pred[2,128,6,128]{1,3,2,0:T(8,128)(4,1)S(1)} %and_bitcast_fusion.2, bf16[4,2,6,128,128]{4,3,2,1,0:T(8,128)(2,1)} %get-tuple-element.154, s32[]{:T(128)} %get-tuple-element.143, bf16[1,2,4,128,128]{4,2,0,3,1:T(4,128)(2,1)S(1)} %constant_dynamic-slice_fusion.2), kind=kOutput, calls=%fused_computation.5.clone.1 | convolution fusion | flops 203684864 | bytes 4002304 | tf_op jit(solution)/shard_map/while/body/eval_jaxpr/bgqd,bskd->bgqsk/dot_general | solution.py:58
  74.3 0.7 fusion.23
  75.0 2.2 %fusion.24 = f32[4,2,4,128,128]{4,3,2,1,0:T(8,128)S(1)} fusion(f32[4,2,4,128,128]{4,3,2,1,0:T(8,128)S(1)} %get-tuple-element.144, s32[]{:T(128)} %get-tuple-element.143, f32[2,4,128,6,128]{2,4,3,1,0:T(8,128)S(1)} %get-tuple-element.133, f32[2,4,128]{2,1,0:T(4,128)S(1)} %fusion.23, f32[2,4,128]{2,1,0:T(4,128)S(1)} %get-tuple-element.134, ...), kind=kOutput, calls=%fused_computation.9.clone.1 | convolution fusion | flops 205258752 | bytes 4269056 | tf_op jit(solution)/shard_map/while/body/eval_jaxpr/bgqsk,bskd->bgqd/dot_general | solution.py:66
  77.2 0.1 constant_dynamic-slice_fusion.2
  77.3 0.2 and_bitcast_fusion.2
  77.5 1.6 %fusion.22 = (f32[2,4,128]{2,1,0:T(4,128)S(1)}, f32[2,4,128,6,128]{2,4,3,1,0:T(8,128)S(1)}) fusion(pred[2,128,6,128]{1,3,2,0:T(8,128)(4,1)S(1)} %and_bitcast_fusion.2, bf16[4,2,6,128,128]{4,3,2,1,0:T(8,128)(2,1)} %get-tuple-element.154, s32[]{:T(128)} %get-tuple-element.143, bf16[1,2,4,128,128]{4,2,0,3,1:T(4,128)(2,1)S(1)} %constant_dynamic-slice_fusion.2), kind=kOutput, calls=%fused_computation.5.clone.1 | convolution fusion | flops 203684864 | bytes 4002304 | tf_op jit(solution)/shard_map/while/body/eval_jaxpr/bgqd,bskd->bgqsk/dot_general | solution.py:58
  79.1 0.7 fusion.23
  79.8 2.2 %fusion.24 = f32[4,2,4,128,128]{4,3,2,1,0:T(8,128)S(1)} fusion(f32[4,2,4,128,128]{4,3,2,1,0:T(8,128)S(1)} %get-tuple-element.144, s32[]{:T(128)} %get-tuple-element.143, f32[2,4,128,6,128]{2,4,3,1,0:T(8,128)S(1)} %get-tuple-element.133, f32[2,4,128]{2,1,0:T(4,128)S(1)} %fusion.23, f32[2,4,128]{2,1,0:T(4,128)S(1)} %get-tuple-element.134, ...), kind=kOutput, calls=%fused_computation.9.clone.1 | convolution fusion | flops 205258752 | bytes 4269056 | tf_op jit(solution)/shard_map/while/body/eval_jaxpr/bgqsk,bskd->bgqd/dot_general | solution.py:66
  81.9 0.1 constant_dynamic-slice_fusion.2
  82.0 0.2 and_bitcast_fusion.2
  82.2 1.6 %fusion.22 = (f32[2,4,128]{2,1,0:T(4,128)S(1)}, f32[2,4,128,6,128]{2,4,3,1,0:T(8,128)S(1)}) fusion(pred[2,128,6,128]{1,3,2,0:T(8,128)(4,1)S(1)} %and_bitcast_fusion.2, bf16[4,2,6,128,128]{4,3,2,1,0:T(8,128)(2,1)} %get-tuple-element.154, s32[]{:T(128)} %get-tuple-element.143, bf16[1,2,4,128,128]{4,2,0,3,1:T(4,128)(2,1)S(1)} %constant_dynamic-slice_fusion.2), kind=kOutput, calls=%fused_computation.5.clone.1 | convolution fusion | flops 203684864 | bytes 4002304 | tf_op jit(solution)/shard_map/while/body/eval_jaxpr/bgqd,bskd->bgqsk/dot_general | solution.py:58
  83.8 0.7 fusion.23
  84.5 2.2 %fusion.24 = f32[4,2,4,128,128]{4,3,2,1,0:T(8,128)S(1)} fusion(f32[4,2,4,128,128]{4,3,2,1,0:T(8,128)S(1)} %get-tuple-element.144, s32[]{:T(128)} %get-tuple-element.143, f32[2,4,128,6,128]{2,4,3,1,0:T(8,128)S(1)} %get-tuple-element.133, f32[2,4,128]{2,1,0:T(4,128)S(1)} %fusion.23, f32[2,4,128]{2,1,0:T(4,128)S(1)} %get-tuple-element.134, ...), kind=kOutput, calls=%fused_computation.9.clone.1 | convolution fusion | flops 205258752 | bytes 4269056 | tf_op jit(solution)/shard_map/while/body/eval_jaxpr/bgqsk,bskd->bgqd/dot_general | solution.py:66
  86.7 0.1 constant_dynamic-slice_fusion.2
  86.8 0.2 and_bitcast_fusion.2
  87.0 1.6 %fusion.22 = (f32[2,4,128]{2,1,0:T(4,128)S(1)}, f32[2,4,128,6,128]{2,4,3,1,0:T(8,128)S(1)}) fusion(pred[2,128,6,128]{1,3,2,0:T(8,128)(4,1)S(1)} %and_bitcast_fusion.2, bf16[4,2,6,128,128]{4,3,2,1,0:T(8,128)(2,1)} %get-tuple-element.154, s32[]{:T(128)} %get-tuple-element.143, bf16[1,2,4,128,128]{4,2,0,3,1:T(4,128)(2,1)S(1)} %constant_dynamic-slice_fusion.2), kind=kOutput, calls=%fused_computation.5.clone.1 | convolution fusion | flops 203684864 | bytes 4002304 | tf_op jit(solution)/shard_map/while/body/eval_jaxpr/bgqd,bskd->bgqsk/dot_general | solution.py:58
  88.5 0.7 fusion.23
  89.2 2.2 %fusion.24 = f32[4,2,4,128,128]{4,3,2,1,0:T(8,128)S(1)} fusion(f32[4,2,4,128,128]{4,3,2,1,0:T(8,128)S(1)} %get-tuple-element.144, s32[]{:T(128)} %get-tuple-element.143, f32[2,4,128,6,128]{2,4,3,1,0:T(8,128)S(1)} %get-tuple-element.133, f32[2,4,128]{2,1,0:T(4,128)S(1)} %fusion.23, f32[2,4,128]{2,1,0:T(4,128)S(1)} %get-tuple-element.134, ...), kind=kOutput, calls=%fused_computation.9.clone.1 | convolution fusion | flops 205258752 | bytes 4269056 | tf_op jit(solution)/shard_map/while/body/eval_jaxpr/bgqsk,bskd->bgqd/dot_general | solution.py:66
  91.4 0.2 multiply_reduce_fusion
  91.6 2.7 %copy.26 = f32[2,128,4,4,128]{4,3,2,1,0:T(4,128)} copy(f32[2,128,4,4,128]{4,1,3,0,2:T(8,128)S(1)} %bitcast.55) | data formatting | bytes 4194304 | tf_op jit(solution)/shard_map/transpose | solution.py:71
  94.3 0.0 copy-start
  94.3 2.1 %reshape.51 = f32[256,2048]{1,0:T(8,128)S(1)} reshape(f32[2,128,4,4,128]{4,3,2,1,0:T(4,128)} %copy.26) | data formatting | bytes 4194304 | tf_op jit(solution)/shard_map/reshape | solution.py:71
  96.5 3.7 %psum.7 = f32[256]{0:T(256)S(1)} all-reduce(f32[256]{0:T(256)S(1)} %bitcast.58), channel_id=1, replica_groups=mesh['ctx'=16,'head'=2] {'head'}, use_global_device_ids=true, to_apply=%region_5.6 | all-reduce | flops 256 | bytes 2048 | tf_op jit(solution)/shard_map/psum | solution.py:73
  100.1 0.0 copy-done
  100.1 1.2 %multiply_convert_fusion = bf16[256,2048]{1,0:T(8,128)(2,1)} fusion(f32[256,2048]{1,0:T(8,128)S(1)} %reshape.51, f32[2048]{0:T(1024)S(1)} %copy-done, f32[256]{0:T(256)S(1)} %add_rsqrt_fusion), kind=kLoop, calls=%fused_computation.22 | loop fusion | flops 1572864 | bytes 3154944 | tf_op jit(solution)/shard_map/convert_element_type | solution.py:75
  (6 shorter events, 0.0 us)
Async XLA Ops:
  0.0 15.0 %collective-permute-start = (bf16[2,256,512]{2,1,0:T(8,128)(2,1)}, bf16[2,256,512]{2,1,0:T(8,128)(2,1)}, u32[]{:S(2)}, u32[]{:S(2)}) collective-permute-start(bf16[2,256,512]{2,1,0:T(8,128)(2,1)} %param.10), channel_id=1, source_target_pairs={{0,2},{2,4},{4,6},{6,8},{8,10},{10,12},{12,14},{14,16},{16,18},{18... | collective-permute-start | bytes 1572872 | tf_op jit(solution)/shard_map/ppermute | solution.py:15
  1.3 29.9 %collective-permute-start.1 = (bf16[2,256,512]{2,1,0:T(8,128)(2,1)}, bf16[2,256,512]{2,1,0:T(8,128)(2,1)}, u32[]{:S(2)}, u32[]{:S(2)}) collective-permute-start(bf16[2,256,512]{2,1,0:T(8,128)(2,1)} %param.10), channel_id=1, source_target_pairs={{0,4},{2,6},{4,8},{6,10},{8,12},{10,14},{12,16},{14,18},{16,20},{1... | collective-permute-start | bytes 1572872 | tf_op jit(solution)/shard_map/ppermute | solution.py:15
  2.6 39.6 %collective-permute-start.2 = (bf16[2,256,512]{2,1,0:T(8,128)(2,1)}, bf16[2,256,512]{2,1,0:T(8,128)(2,1)}, u32[]{:S(2)}, u32[]{:S(2)}) collective-permute-start(bf16[2,256,512]{2,1,0:T(8,128)(2,1)} %param.10), channel_id=1, source_target_pairs={{0,8},{2,10},{4,12},{6,14},{8,16},{10,18},{12,20},{14,22},{16,24},... | collective-permute-start | bytes 1572872 | tf_op jit(solution)/shard_map/ppermute | solution.py:15
  3.9 60.7 %collective-permute-start.3 = (bf16[2,256,512]{2,1,0:T(8,128)(2,1)}, bf16[2,256,512]{2,1,0:T(8,128)(2,1)}, u32[]{:S(2)}, u32[]{:S(2)}) collective-permute-start(bf16[2,256,512]{2,1,0:T(8,128)(2,1)} %param.10), channel_id=1, source_target_pairs={{0,16},{2,18},{4,20},{6,22},{8,24},{10,26},{12,28},{14,30},{1,17},... | collective-permute-start | bytes 1572872 | tf_op jit(solution)/shard_map/ppermute | solution.py:15
  94.3 5.8 %copy-start = (f32[2048]{0:T(1024)S(1)}, f32[2048]{0:T(1024)}, u32[]{:S(2)}) copy-start(f32[2048]{0:T(1024)} %param.11) | copy-start | bytes 24580
where the time goes:
time: 103 us; the launch traced here: 101 us
  local copies, waits for them, and re-layouts  36.7 us (36%)
  waiting for transfers between devices  32 us (31%)
  matrix products  15 us (15%)
  other arithmetic  8.63 us (8%)
  starting transfers between devices  5.16 us (5%)
  blocking collectives  3.68 us (4%)
    ppermute x4, waiting for transfers between devices, shifted(): lax.ppermute(value, axis, [(source, source + steps) for source in range(f...  32 us
    dot_general x4, matrix products, attend_head(): jnp.einsum('bgqsk,bskd->bgqd', probabilities, value_head, preferred_eleme...  8.65 us
    unnamed x6, local copies, waits for them, and re-layouts  8.39 us
    another operation x4, local copies, waits for them, and re-layouts, local(): jnp.stack([panel.reshape(2, blocks, BLK, kv_local, HD) for panel in panel...  7.83 us
    dot_general x4, matrix products, attend_head(): jnp.einsum('bgqd,bskd->bgqsk', query_head, key_head, preferred_element_ty...  6.34 us
    ppermute x4, starting transfers between devices, shifted(): lax.ppermute(value, axis, [(source, source + steps) for source in range(f...  5.16 us
    reshape x2, local copies, waits for them, and re-layouts, local(): jnp.concatenate([panels[0], keyval], axis=1)  4.61 us
    transpose x1, local copies, waits for them, and re-layouts, local(): value_heads = selected[1].transpose(3, 0, 1, 2, 4)  4 us
  transfers between devices with their start and end apart: 4, of which 3 were waited for; matrix products, arithmetic and copies ran while one was open for 27% of the time, Pallas kernels for 0%

commit v1 on v0

v1 whole, which is shorter than its diff:
```python
import functools
import math

import jax
import jax.numpy as jnp
from jax import lax
from jax.experimental import pallas as pl
from jax.experimental.pallas import tpu as pltpu
from jax.sharding import PartitionSpec as P

HD = 128
BLK = 128
MESH = pl.DeviceIdType.MESH
F32 = jnp.float32
BF16 = jnp.bfloat16


def kernel(
    ctx, levels, kvh, group, features,
    q_hbm, kv_hbm, gain_ref, out_ref,
    kvbuf, qbuf, acc, mbuf, ssq, ssq_peer,
    qsem, kvsem, send_sem, recv_sem, nsend, nrecv,
):
    p = lax.axis_index("ctx")
    core = lax.axis_index("head")
    c = HD ** (-0.5) * math.log2(math.e)
    rows = group * BLK
    bit0 = lax.rem(p, 2)
    bit1 = lax.rem(p // 2, 2)

    def kv_load(h):
        return pltpu.make_async_copy(
            kv_hbm.at[:, :, pl.ds(h * HD, HD)], kvbuf.at[0, h], kvsem.at[h]
        )

    def q_load(h):
        return pltpu.make_async_copy(
            q_hbm.at[:, pl.ds(h * HD, HD)], qbuf.at[h], qsem.at[h]
        )

    for h in range(kvh):
        kv_load(h).start()
    for h in range(kvh * group):
        q_load(h).start()

    barrier = pltpu.get_barrier_semaphore()
    shifts = [1, 2, 4] + [2**k for k in range(4, levels)]
    expect = jnp.int32(1)
    pl.semaphore_signal(barrier, inc=1, device_id={"head": 1 - core}, device_id_type=MESH)
    for s in shifts:
        up = p + s < ctx
        down = p >= s

        @pl.when(up)
        def _():
            pl.semaphore_signal(barrier, inc=1, device_id={"ctx": p + s}, device_id_type=MESH)

        @pl.when(down)
        def _():
            pl.semaphore_signal(barrier, inc=1, device_id={"ctx": p - s}, device_id_type=MESH)

        expect = expect + up.astype(jnp.int32) + down.astype(jnp.int32)
    pl.semaphore_wait(barrier, expect)

    def send(src, dst, kind, h, target):
        return pltpu.make_async_remote_copy(
            src_ref=kvbuf.at[src, h],
            dst_ref=kvbuf.at[dst, h],
            send_sem=send_sem.at[kind, h],
            recv_sem=recv_sem.at[dst - 1, h],
            device_id={"ctx": target},
            device_id_type=MESH,
        )

    own_sends = [
        (p + 4 < ctx, 0, 3, 2, p + 4),
        (bit1 == 0, 0, 2, 1, p + 2),
        (bit0 == 0, 0, 1, 0, p + 1),
    ] + [(p + 2**k < ctx, 0, k + 1, k + 2, p + 2**k) for k in range(4, levels)]
    from_l2 = [
        (jnp.logical_and(p >= 4, p + 4 < ctx), 3, 4, 4, p + 4),
        (jnp.logical_and(p >= 4, bit1 == 1), 3, 2, 3, p - 2),
    ]
    from_l1 = [(jnp.logical_and(p >= 2, bit0 == 1), 2, 1, 5, p - 1)]

    def start(plan, h):
        for cond, src, dst, kind, target in plan:

            @pl.when(cond)
            def _():
                send(src, dst, kind, h, target).start()

    def arrived(level, h):
        send(0, level + 1, 0, h, p + 1 - 2 * bit0).wait_recv()

    for h in range(kvh):
        kv_load(h).wait()
        start(own_sends, h)

    ones = jnp.ones((2 * BLK, HD), BF16)
    lower = (
        lax.broadcasted_iota(jnp.int32, (group, BLK, BLK), 1)
        >= lax.broadcasted_iota(jnp.int32, (group, BLK, BLK), 2)
    ).reshape(rows, BLK)

    def step(h, b, slot, lo, nk, first=False, full=-1):
        idx = h * 2 + b
        q = qbuf[pl.ds(h * group, group), b * BLK : (b + 1) * BLK, :].reshape(rows, HD)
        k = kvbuf[slot, h, 0, lo : lo + nk, :]
        v = kvbuf[slot, h, 1, lo : lo + nk, :]
        s = lax.dot_general(q, k, (((1,), (1,)), ((), ())), preferred_element_type=F32)
        parts = [s[:, i : i + BLK] for i in range(0, nk, BLK)]
        parts = [x if i == full else jnp.where(lower, x, -jnp.inf) for i, x in enumerate(parts)]
        top = functools.reduce(jnp.maximum, parts)
        top = jnp.broadcast_to(jnp.max(top, axis=1, keepdims=True), (rows, BLK))
        if not first:
            old = mbuf[idx]
            top = jnp.maximum(old, top)
        w = jnp.concatenate([jnp.exp2((x - top) * c).astype(BF16) for x in parts], axis=1)
        pv = jnp.dot(
            w, jnp.concatenate([v, ones[:nk]], axis=1), preferred_element_type=F32
        )
        mbuf[idx] = top
        if first:
            acc[idx] = pv
        else:
            alpha = jnp.exp2((old - top) * c)
            acc[idx] = acc[idx] * jnp.concatenate([alpha, alpha], axis=1) + pv

    for h in range(kvh * group):
        q_load(h).wait()

    @pl.loop(0, kvh)
    def _(h):
        step(h, 0, 0, 0, BLK, first=True, full=0)
        step(h, 1, 0, 0, 2 * BLK, first=True, full=1)

    @pl.loop(0, kvh + 2)
    def _(i):
        @pl.when(jnp.logical_and(i < kvh, p >= 4))
        def _():
            arrived(2, i)
            start(from_l2, i)

        h1 = jnp.maximum(i - 1, 0)
        on1 = jnp.logical_and(jnp.logical_and(i >= 1, i <= kvh), p >= 2)

        @pl.when(on1)
        def _():
            arrived(1, h1)
            start(from_l1, h1)

        @pl.when(jnp.logical_and(i < kvh, p >= 4))
        def _():
            step(i, 0, 3, 0, BLK)
            step(i, 1, 3, BLK, BLK)

        @pl.when(on1)
        def _():
            step(h1, 0, 2, 0, BLK)
            step(h1, 1, 2, BLK, BLK)

        h0 = jnp.maximum(i - 2, 0)

        @pl.when(jnp.logical_and(i >= 2, p >= 1))
        def _():
            arrived(0, h0)
            step(h0, 0, 1, 0, 2 * BLK)
            step(h0, 1, 1, BLK, BLK)

    ssq[...] = jnp.zeros_like(ssq)

    @pl.loop(0, kvh)
    def _(h):
        for k in range(3, levels):

            @pl.when(p >= 2**k)
            def _():
                arrived(k, h)
                step(h, 0, k + 1, 0, BLK)
                step(h, 1, k + 1, BLK, BLK)

        for b in range(2):
            idx = h * 2 + b
            o = acc[idx, :, :HD] * (1.0 / acc[idx, :, HD:])
            acc[idx, :, :HD] = o
            ssq[b] += jnp.sum((o * o).reshape(group, BLK, HD), axis=0)

    swap = pltpu.make_async_remote_copy(
        src_ref=ssq, dst_ref=ssq_peer, send_sem=nsend, recv_sem=nrecv,
        device_id={"head": 1 - core}, device_id_type=MESH,
    )
    swap.start()

    def drain(plan, h):
        for cond, src, dst, kind, target in plan:

            @pl.when(cond)
            def _():
                send(src, dst, kind, h, target).wait_send()

    for h in range(kvh):
        drain(own_sends + from_l2 + from_l1, h)
    swap.wait()

    for b in range(2):
        total = jnp.sum(ssq[b] + ssq_peer[b], axis=1, keepdims=True)
        inv = jnp.broadcast_to(lax.rsqrt(total / features + 1e-06), (BLK, HD))
        for h in range(kvh):
            for g in range(group):
                cols = slice((h * group + g) * HD, (h * group + g + 1) * HD)
                o = acc[h * 2 + b, g * BLK : (g + 1) * BLK, :HD]
                out_ref[b * BLK : (b + 1) * BLK, cols] = (o * inv * gain_ref[:, cols]).astype(BF16)


def local(queries, keyval, out_gain):
    ctx = lax.axis_size("ctx")
    levels = ctx.bit_length() - 1
    toks = queries.shape[0]
    kvh = keyval.shape[2] // HD
    heads = queries.shape[1] // HD
    group = heads // kvh
    features = queries.shape[1] * lax.axis_size("head")
    kinds = max(6, levels + 2)
    body = functools.partial(kernel, ctx, levels, kvh, group, features)
    return pl.pallas_call(
        body,
        out_shape=jax.ShapeDtypeStruct(queries.shape, BF16),
        in_specs=[
            pl.BlockSpec(memory_space=pltpu.HBM),
            pl.BlockSpec(memory_space=pltpu.HBM),
            pl.BlockSpec(memory_space=pltpu.VMEM),
        ],
        out_specs=pl.BlockSpec(memory_space=pltpu.VMEM),
        scratch_shapes=[
            pltpu.VMEM((levels + 1, kvh, 2, toks, HD), BF16),
            pltpu.VMEM((heads, toks, HD), BF16),
            pltpu.VMEM((kvh * 2, group * BLK, 2 * HD), F32),
            pltpu.VMEM((kvh * 2, group * BLK, HD), F32),
            pltpu.VMEM((2, BLK, HD), F32),
            pltpu.VMEM((2, BLK, HD), F32),
            pltpu.SemaphoreType.DMA((heads,)),
            pltpu.SemaphoreType.DMA((kvh,)),
            pltpu.SemaphoreType.DMA((kinds, kvh)),
            pltpu.SemaphoreType.DMA((levels, kvh)),
            pltpu.SemaphoreType.DMA,
            pltpu.SemaphoreType.DMA,
        ],
        compiler_params=pltpu.CompilerParams(
            collective_id=0, has_side_effects=True, vmem_limit_bytes=40 * 2**20
        ),
        cost_estimate=pl.CostEstimate(
            flops=2 * 2 * 2 * BLK * BLK * HD * heads * (levels + 2),
            bytes_accessed=4 * 2**20,
            transcendentals=2 * BLK * BLK * heads * (levels + 2),
        ),
    )(queries, keyval, out_gain.reshape(1, -1))


def solution(mesh):
    in_specs = (P("ctx", "head"), P(None, "ctx", "head"), P("head"))
    out_specs = P("ctx", "head")
    return jax.shard_map(local, mesh=mesh, in_specs=in_specs, out_specs=out_specs, check_vma=False)
```

time: 103 us -> 35.6 us (0.35)
  the two profiles are of different devices: /device:TPU:31 before, /device:TPU:17 now
where the time goes in v1:
time: 35.6 us; the launch traced here: 35.4 us
  Pallas kernels  31.5 us (88%)
  local copies, waits for them, and re-layouts  3.93 us (11%)
    pallas_call x1, Pallas kernels, local(): pl.pallas_call(body, out_shape=jax.ShapeDtypeStruct(queries.shape, BF16),...  31.5 us
    unnamed x7, local copies, waits for them, and re-layouts  3.93 us

profile of v1, /device:TPU:17, one launch (start us, length us, event | category | flops | bytes accessed | tf_op | source)
XLA Modules:
  0.0 35.4 jit_solution(13661341844680689851)
XLA Ops:
  0.0 0.0 copy-start
  0.0 1.2 %copy-done = bf16[256,2048]{1,0:T(8,128)(2,1)S(1)} copy-done((bf16[256,2048]{1,0:T(8,128)(2,1)S(1)}, bf16[256,2048]{1,0:T(8,128)(2,1)}, u32[]{:S(2)}) %copy-start) | copy-done | bytes 1048600
  1.2 0.0 copy-start.1
  1.2 1.0 %copy-done.1 = bf16[2,256,512]{2,1,0:T(8,128)(2,1)S(1)} copy-done((bf16[2,256,512]{2,1,0:T(8,128)(2,1)S(1)}, bf16[2,256,512]{2,1,0:T(8,128)(2,1)}, u32[]{:S(2)}) %copy-start.1) | copy-done | bytes 524312
  2.3 0.0 copy-start.2
  2.3 0.7 %copy-done.2 = f32[2048]{0:T(1024)S(1)} copy-done((f32[2048]{0:T(1024)S(1)}, f32[2048]{0:T(1024)}, u32[]{:S(2)}) %copy-start.2) | copy-done | bytes 8216
  3.0 31.5 %shard_map.37 = bf16[256,2048]{1,0:T(8,128)(2,1)S(1)} custom-call(bf16[256,2048]{1,0:T(8,128)(2,1)S(1)} %copy-done, bf16[2,256,512]{2,1,0:T(8,128)(2,1)S(1)} %copy-done.1, f32[1,2048]{1,0:T(1,128)S(1)} %bitcast.1), custom_call_target="tpu_custom_call" | custom-call | flops 1610612736 | bytes 4194304 | tf_op jit(solution)/shard_map/pallas_call | solution.py:226
  34.4 1.0 %copy.5 = bf16[256,2048]{1,0:T(8,128)(2,1)} copy(bf16[256,2048]{1,0:T(8,128)(2,1)S(1)} %shard_map.37) | data formatting | bytes 2097152
Async XLA Ops:
  0.0 1.2 %copy-start = (bf16[256,2048]{1,0:T(8,128)(2,1)S(1)}, bf16[256,2048]{1,0:T(8,128)(2,1)}, u32[]{:S(2)}) copy-start(bf16[256,2048]{1,0:T(8,128)(2,1)} %q_hbm.1) | copy-start | bytes 3145732
  1.2 1.0 %copy-start.1 = (bf16[2,256,512]{2,1,0:T(8,128)(2,1)S(1)}, bf16[2,256,512]{2,1,0:T(8,128)(2,1)}, u32[]{:S(2)}) copy-start(bf16[2,256,512]{2,1,0:T(8,128)(2,1)} %kv_hbm.1) | copy-start | bytes 1572868
  2.3 0.7 %copy-start.2 = (f32[2048]{0:T(1024)S(1)}, f32[2048]{0:T(1024)}, u32[]{:S(2)}) copy-start(f32[2048]{0:T(1024)} %param.5) | copy-start | bytes 24580

commit v2 on v1

--- a/solution.py
+++ b/solution.py
@@ -11,15 +11,16 @@
 HD = 128
 BLK = 128
 MESH = pl.DeviceIdType.MESH
+VMEM_LIMIT = 56 * 2**20
 F32 = jnp.float32
 BF16 = jnp.bfloat16
 
 
 def kernel(
     ctx, levels, kvh, group, features,
-    q_hbm, kv_hbm, gain_ref, out_ref,
-    kvbuf, qbuf, acc, mbuf, ssq, ssq_peer,
-    qsem, kvsem, send_sem, recv_sem, nsend, nrecv,
+    q_hbm, kv_hbm, gain_ref, out_hbm,
+    kvbuf, qbuf, acc, mbuf, ssq, ssq_peer, obuf,
+    qsem, kvsem, send_sem, recv_sem, nsend, nrecv, osem,
 ):
     p = lax.axis_index("ctx")
     core = lax.axis_index("head")
@@ -77,10 +78,8 @@
         (bit1 == 0, 0, 2, 1, p + 2),
         (bit0 == 0, 0, 1, 0, p + 1),
     ] + [(p + 2**k < ctx, 0, k + 1, k + 2, p + 2**k) for k in range(4, levels)]
-    from_l2 = [
-        (jnp.logical_and(p >= 4, p + 4 < ctx), 3, 4, 4, p + 4),
-        (jnp.logical_and(p >= 4, bit1 == 1), 3, 2, 3, p - 2),
-    ]
+    onward = [(jnp.logical_and(p >= 4, p + 4 < ctx), 3, 4, 4, p + 4)]
+    from_l2 = [(jnp.logical_and(p >= 4, bit1 == 1), 3, 2, 3, p - 2)]
     from_l1 = [(jnp.logical_and(p >= 2, bit0 == 1), 2, 1, 5, p - 1)]
 
     def start(plan, h):
@@ -93,9 +92,17 @@
     def arrived(level, h):
         send(0, level + 1, 0, h, p + 1 - 2 * bit0).wait_recv()
 
+    def drain(plan, h):
+        for cond, src, dst, kind, target in plan:
+
+            @pl.when(cond)
+            def _():
+                send(src, dst, kind, h, target).wait_send()
+
     for h in range(kvh):
         kv_load(h).wait()
-        start(own_sends, h)
+        if h < 2:
+            start(own_sends, h)
 
     ones = jnp.ones((2 * BLK, HD), BF16)
     lower = (
@@ -137,10 +144,26 @@
 
     @pl.loop(0, kvh + 2)
     def _(i):
+        @pl.when(i < kvh)
+        def _():
+            drain(own_sends, i)
+
+        @pl.when(i < kvh - 2)
+        def _():
+            start(own_sends, i + 2)
+
         @pl.when(jnp.logical_and(i < kvh, p >= 4))
         def _():
             arrived(2, i)
             start(from_l2, i)
+
+        @pl.when(i >= kvh)
+        def _():
+            drain(onward, i - kvh)
+
+        @pl.when(i >= kvh - 2)
+        def _():
+            start(onward, i - (kvh - 2))
 
         h1 = jnp.maximum(i - 1, 0)
         on1 = jnp.logical_and(jnp.logical_and(i >= 1, i <= kvh), p >= 2)
@@ -192,16 +215,15 @@
     )
     swap.start()
 
-    def drain(plan, h):
-        for cond, src, dst, kind, target in plan:
-
-            @pl.when(cond)
-            def _():
-                send(src, dst, kind, h, target).wait_send()
-
     for h in range(kvh):
-        drain(own_sends + from_l2 + from_l1, h)
+        if h >= 2:
+            drain(onward, h)
+        drain(from_l2 + from_l1, h)
     swap.wait()
+
+    def store(b, h):
+        part = (pl.ds(b * BLK, BLK), pl.ds(h * group * HD, group * HD))
+        return pltpu.make_async_copy(obuf.at[part], out_hbm.at[part], osem.at[b, h])
 
     for b in range(2):
         total = jnp.sum(ssq[b] + ssq_peer[b], axis=1, keepdims=True)
@@ -210,7 +232,11 @@
             for g in range(group):
                 cols = slice((h * group + g) * HD, (h * group + g + 1) * HD)
                 o = acc[h * 2 + b, g * BLK : (g + 1) * BLK, :HD]
-                out_ref[b * BLK : (b + 1) * BLK, cols] = (o * inv * gain_ref[:, cols]).astype(BF16)
+                obuf[b * BLK : (b + 1) * BLK, cols] = (o * inv * gain_ref[:, cols]).astype(BF16)
+            store(b, h).start()
+    for b in range(2):
+        for h in range(kvh):
+            store(b, h).wait()
 
 
 def local(queries, keyval, out_gain):
@@ -231,7 +257,7 @@
             pl.BlockSpec(memory_space=pltpu.HBM),
             pl.BlockSpec(memory_space=pltpu.VMEM),
         ],
-        out_specs=pl.BlockSpec(memory_space=pltpu.VMEM),
+        out_specs=pl.BlockSpec(memory_space=pltpu.HBM),
         scratch_shapes=[
             pltpu.VMEM((levels + 1, kvh, 2, toks, HD), BF16),
             pltpu.VMEM((heads, toks, HD), BF16),
@@ -239,15 +265,17 @@
             pltpu.VMEM((kvh * 2, group * BLK, HD), F32),
             pltpu.VMEM((2, BLK, HD), F32),
             pltpu.VMEM((2, BLK, HD), F32),
+            pltpu.VMEM(queries.shape, BF16),
             pltpu.SemaphoreType.DMA((heads,)),
             pltpu.SemaphoreType.DMA((kvh,)),
             pltpu.SemaphoreType.DMA((kinds, kvh)),
             pltpu.SemaphoreType.DMA((levels, kvh)),
             pltpu.SemaphoreType.DMA,
             pltpu.SemaphoreType.DMA,
+            pltpu.SemaphoreType.DMA((2, kvh)),
         ],
         compiler_params=pltpu.CompilerParams(
-            collective_id=0, has_side_effects=True, vmem_limit_bytes=40 * 2**20
+            collective_id=0, has_side_effects=True, vmem_limit_bytes=VMEM_LIMIT
         ),
         cost_estimate=pl.CostEstimate(
             flops=2 * 2 * 2 * BLK * BLK * HD * heads * (levels + 2),

time: 35.6 us -> 35.2 us (0.989)
  local copies, waits for them, and re-layouts: 3.93 us -> 2.3 us
  Pallas kernels: 31.5 us -> 32.7 us
    unnamed x7 -> x1, local copies, waits for them, and re-layouts: 3.93 us -> 2.3 us
    pallas_call x1, Pallas kernels: 31.5 us -> 32.7 us  [local(): pl.pallas_call(body, out_shape=jax.ShapeDtypeStruct(queries.shape, BF16),...]
where the time goes in v2:
time: 35.2 us; the launch traced here: 35 us
  Pallas kernels  32.7 us (93%)
  local copies, waits for them, and re-layouts  2.3 us (7%)
    pallas_call x1, Pallas kernels, local(): pl.pallas_call(body, out_shape=jax.ShapeDtypeStruct(queries.shape, BF16),...  32.7 us
    unnamed x1, local copies, waits for them, and re-layouts  2.3 us

profile of v2, /device:TPU:17, one launch (start us, length us, event | category | flops | bytes accessed | tf_op | source)
XLA Modules:
  0.0 35.0 jit_solution(7843429237487832460)
XLA Ops:
  0.0 32.7 %shard_map.37 = bf16[256,2048]{1,0:T(8,128)(2,1)} custom-call(bf16[256,2048]{1,0:T(8,128)(2,1)} %q_hbm.1, bf16[2,256,512]{2,1,0:T(8,128)(2,1)} %kv_hbm.1, f32[1,2048]{1,0:T(1,128)} %bitcast.1), custom_call_target="tpu_custom_call" | custom-call | flops 1610612736 | bytes 4194304 | tf_op jit(solution)/shard_map/pallas_call | solution.py:252
  32.7 2.3 %copy.5 = bf16[256,2048]{1,0:T(8,128)(2,1)} copy(bf16[256,2048]{1,0:T(8,128)(2,1)} %shard_map.37) | data formatting | bytes 2097152

commit v3 on v1

--- a/solution.py
+++ b/solution.py
@@ -11,15 +11,16 @@
 HD = 128
 BLK = 128
 MESH = pl.DeviceIdType.MESH
+VMEM_LIMIT = 40 * 2**20
 F32 = jnp.float32
 BF16 = jnp.bfloat16
 
 
 def kernel(
     ctx, levels, kvh, group, features,
-    q_hbm, kv_hbm, gain_ref, out_ref,
-    kvbuf, qbuf, acc, mbuf, ssq, ssq_peer,
-    qsem, kvsem, send_sem, recv_sem, nsend, nrecv,
+    q_hbm, kv_hbm, gain_hbm, out_ref,
+    kvbuf, qbuf, acc, mbuf, ssq, ssq_peer, gain,
+    qsem, kvsem, send_sem, recv_sem, nsend, nrecv, gsem,
 ):
     p = lax.axis_index("ctx")
     core = lax.axis_index("head")
@@ -28,9 +29,9 @@
     bit0 = lax.rem(p, 2)
     bit1 = lax.rem(p // 2, 2)
 
-    def kv_load(h):
+    def kv_load(h, half):
         return pltpu.make_async_copy(
-            kv_hbm.at[:, :, pl.ds(h * HD, HD)], kvbuf.at[0, h], kvsem.at[h]
+            kv_hbm.at[half, :, pl.ds(h * HD, HD)], kvbuf.at[0, h, half], kvsem.at[h, half]
         )
 
     def q_load(h):
@@ -39,9 +40,12 @@
         )
 
     for h in range(kvh):
-        kv_load(h).start()
+        for half in range(2):
+            kv_load(h, half).start()
     for h in range(kvh * group):
         q_load(h).start()
+    gain_load = pltpu.make_async_copy(gain_hbm, gain, gsem)
+    gain_load.start()
 
     barrier = pltpu.get_barrier_semaphore()
     shifts = [1, 2, 4] + [2**k for k in range(4, levels)]
@@ -62,12 +66,12 @@
         expect = expect + up.astype(jnp.int32) + down.astype(jnp.int32)
     pl.semaphore_wait(barrier, expect)
 
-    def send(src, dst, kind, h, target):
+    def send(src, dst, kind, h, half, target):
         return pltpu.make_async_remote_copy(
-            src_ref=kvbuf.at[src, h],
-            dst_ref=kvbuf.at[dst, h],
-            send_sem=send_sem.at[kind, h],
-            recv_sem=recv_sem.at[dst - 1, h],
+            src_ref=kvbuf.at[src, h, half],
+            dst_ref=kvbuf.at[dst, h, half],
+            send_sem=send_sem.at[kind, h, half],
+            recv_sem=recv_sem.at[dst - 1, h, half],
             device_id={"ctx": target},
             device_id_type=MESH,
         )
@@ -77,25 +81,31 @@
         (bit1 == 0, 0, 2, 1, p + 2),
         (bit0 == 0, 0, 1, 0, p + 1),
     ] + [(p + 2**k < ctx, 0, k + 1, k + 2, p + 2**k) for k in range(4, levels)]
-    from_l2 = [
-        (jnp.logical_and(p >= 4, p + 4 < ctx), 3, 4, 4, p + 4),
-        (jnp.logical_and(p >= 4, bit1 == 1), 3, 2, 3, p - 2),
-    ]
+    onward = [(jnp.logical_and(p >= 4, p + 4 < ctx), 3, 4, 4, p + 4)]
+    from_l2 = [(jnp.logical_and(p >= 4, bit1 == 1), 3, 2, 3, p - 2)]
     from_l1 = [(jnp.logical_and(p >= 2, bit0 == 1), 2, 1, 5, p - 1)]
 
-    def start(plan, h):
+    def start(plan, h, half):
         for cond, src, dst, kind, target in plan:
 
             @pl.when(cond)
             def _():
-                send(src, dst, kind, h, target).start()
-
-    def arrived(level, h):
-        send(0, level + 1, 0, h, p + 1 - 2 * bit0).wait_recv()
+                send(src, dst, kind, h, half, target).start()
+
+    def drain(plan, h, half):
+        for cond, src, dst, kind, target in plan:
+
+            @pl.when(cond)
+            def _():
+                send(src, dst, kind, h, half, target).wait_send()
+
+    def arrived(level, h, half):
+        send(0, level + 1, 0, h, half, p + 1 - 2 * bit0).wait_recv()
 
     for h in range(kvh):
-        kv_load(h).wait()
-        start(own_sends, h)
+        for half in range(2):
+            kv_load(h, half).wait()
+            start(own_sends, h, half)
 
     ones = jnp.ones((2 * BLK, HD), BF16)
     lower = (
@@ -135,22 +145,35 @@
         step(h, 0, 0, 0, BLK, first=True, full=0)
         step(h, 1, 0, 0, 2 * BLK, first=True, full=1)
 
-    @pl.loop(0, kvh + 2)
+    @pl.loop(0, kvh + 1)
     def _(i):
-        @pl.when(jnp.logical_and(i < kvh, p >= 4))
-        def _():
-            arrived(2, i)
-            start(from_l2, i)
-
         h1 = jnp.maximum(i - 1, 0)
-        on1 = jnp.logical_and(jnp.logical_and(i >= 1, i <= kvh), p >= 2)
-
-        @pl.when(on1)
-        def _():
-            arrived(1, h1)
-            start(from_l1, h1)
-
-        @pl.when(jnp.logical_and(i < kvh, p >= 4))
+        on2 = jnp.logical_and(i < kvh, p >= 4)
+        on1 = jnp.logical_and(i >= 1, p >= 2)
+        for half in range(2):
+
+            @pl.when(on2)
+            def _():
+                arrived(2, i, half)
+                start(from_l2, i, half)
+
+            @pl.when(on1)
+            def _():
+                arrived(1, h1, half)
+                start(from_l1, h1, half)
+
+        @pl.when(jnp.logical_and(i >= 2, i < kvh))
+        def _():
+            for half in range(2):
+                start(onward, i - 2, half)
+
+        @pl.when(i == kvh - 1)
+        def _():
+            for h in range(kvh - 2, kvh):
+                for half in range(2):
+                    start(onward, h, half)
+
+        @pl.when(on2)
         def _():
             step(i, 0, 3, 0, BLK)
             step(i, 1, 3, BLK, BLK)
@@ -160,31 +183,35 @@
             step(h1, 0, 2, 0, BLK)
             step(h1, 1, 2, BLK, BLK)
 
-        h0 = jnp.maximum(i - 2, 0)
-
-        @pl.when(jnp.logical_and(i >= 2, p >= 1))
-        def _():
-            arrived(0, h0)
-            step(h0, 0, 1, 0, 2 * BLK)
-            step(h0, 1, 1, BLK, BLK)
-
     ssq[...] = jnp.zeros_like(ssq)
+    gain_load.wait()
 
     @pl.loop(0, kvh)
     def _(h):
+        @pl.when(p >= 1)
+        def _():
+            arrived(0, h, 0)
+            arrived(0, h, 1)
+            step(h, 0, 1, 0, 2 * BLK)
+            step(h, 1, 1, BLK, BLK)
+
         for k in range(3, levels):
 
             @pl.when(p >= 2**k)
             def _():
-                arrived(k, h)
+                arrived(k, h, 0)
+                arrived(k, h, 1)
                 step(h, 0, k + 1, 0, BLK)
                 step(h, 1, k + 1, BLK, BLK)
 
         for b in range(2):
             idx = h * 2 + b
             o = acc[idx, :, :HD] * (1.0 / acc[idx, :, HD:])
-            acc[idx, :, :HD] = o
             ssq[b] += jnp.sum((o * o).reshape(group, BLK, HD), axis=0)
+            for g in range(group):
+                acc[idx, g * BLK : (g + 1) * BLK, :HD] = (
+                    o[g * BLK : (g + 1) * BLK] * gain[pl.ds(h * group + g, 1), :]
+                )
 
     swap = pltpu.make_async_remote_copy(
         src_ref=ssq, dst_ref=ssq_peer, send_sem=nsend, recv_sem=nrecv,
@@ -192,15 +219,9 @@
     )
     swap.start()
 
-    def drain(plan, h):
-        for cond, src, dst, kind, target in plan:
-
-            @pl.when(cond)
-            def _():
-                send(src, dst, kind, h, target).wait_send()
-
     for h in range(kvh):
-        drain(own_sends + from_l2 + from_l1, h)
+        for half in range(2):
+            drain(own_sends + onward + from_l2 + from_l1, h, half)
     swap.wait()
 
     for b in range(2):
@@ -210,7 +231,7 @@
             for g in range(group):
                 cols = slice((h * group + g) * HD, (h * group + g + 1) * HD)
                 o = acc[h * 2 + b, g * BLK : (g + 1) * BLK, :HD]
-                out_ref[b * BLK : (b + 1) * BLK, cols] = (o * inv * gain_ref[:, cols]).astype(BF16)
+                out_ref[b * BLK : (b + 1) * BLK, cols] = (o * inv).astype(BF16)
 
 
 def local(queries, keyval, out_gain):
@@ -223,13 +244,14 @@
     features = queries.shape[1] * lax.axis_size("head")
     kinds = max(6, levels + 2)
     body = functools.partial(kernel, ctx, levels, kvh, group, features)
+    operands = (queries, keyval, out_gain.reshape(heads, HD))
     return pl.pallas_call(
         body,
         out_shape=jax.ShapeDtypeStruct(queries.shape, BF16),
         in_specs=[
             pl.BlockSpec(memory_space=pltpu.HBM),
             pl.BlockSpec(memory_space=pltpu.HBM),
-            pl.BlockSpec(memory_space=pltpu.VMEM),
+            pl.BlockSpec(memory_space=pltpu.HBM),
         ],
         out_specs=pl.BlockSpec(memory_space=pltpu.VMEM),
         scratch_shapes=[
@@ -239,22 +261,24 @@
             pltpu.VMEM((kvh * 2, group * BLK, HD), F32),
             pltpu.VMEM((2, BLK, HD), F32),
             pltpu.VMEM((2, BLK, HD), F32),
+            pltpu.VMEM((heads, HD), F32),
             pltpu.SemaphoreType.DMA((heads,)),
-            pltpu.SemaphoreType.DMA((kvh,)),
-            pltpu.SemaphoreType.DMA((kinds, kvh)),
-            pltpu.SemaphoreType.DMA((levels, kvh)),
+            pltpu.SemaphoreType.DMA((kvh, 2)),
+            pltpu.SemaphoreType.DMA((kinds, kvh, 2)),
+            pltpu.SemaphoreType.DMA((levels, kvh, 2)),
+            pltpu.SemaphoreType.DMA,
             pltpu.SemaphoreType.DMA,
             pltpu.SemaphoreType.DMA,
         ],
         compiler_params=pltpu.CompilerParams(
-            collective_id=0, has_side_effects=True, vmem_limit_bytes=40 * 2**20
+            collective_id=0, has_side_effects=True, vmem_limit_bytes=VMEM_LIMIT
         ),
         cost_estimate=pl.CostEstimate(
             flops=2 * 2 * 2 * BLK * BLK * HD * heads * (levels + 2),
             bytes_accessed=4 * 2**20,
             transcendentals=2 * BLK * BLK * heads * (levels + 2),
         ),
-    )(queries, keyval, out_gain.reshape(1, -1))
+    )(*(pltpu.with_memory_space_constraint(x, pltpu.HBM) for x in operands))
 
 
 def solution(mesh):

time: 35.6 us -> 30.5 us (0.86)
  local copies, waits for them, and re-layouts: 3.93 us -> 0.97 us
  Pallas kernels: 31.5 us -> 29.4 us
    unnamed x7 -> x1, local copies, waits for them, and re-layouts: 3.93 us -> 0.97 us
    pallas_call x1, Pallas kernels: 31.5 us -> 29.4 us  [local(): pl.pallas_call(body, out_shape=jax.ShapeDtypeStruct(queries.shape, BF16),...]
where the time goes in v3:
time: 30.5 us; the launch traced here: 30.4 us
  Pallas kernels  29.4 us (96%)
  local copies, waits for them, and re-layouts  0.97 us (3%)
    pallas_call x1, Pallas kernels, local(): pl.pallas_call(body, out_shape=jax.ShapeDtypeStruct(queries.shape, BF16),...  29.4 us
    unnamed x1, local copies, waits for them, and re-layouts  0.97 us

profile of v3, /device:TPU:17, one launch (start us, length us, event | category | flops | bytes accessed | tf_op | source)
XLA Modules:
  0.0 30.4 jit_solution(13938856361622150977)
XLA Ops:
  0.0 29.4 %shard_map.37 = bf16[256,2048]{1,0:T(8,128)(2,1)S(1)} custom-call(bf16[256,2048]{1,0:T(8,128)(2,1)} %q_hbm.1, bf16[2,256,512]{2,1,0:T(8,128)(2,1)} %kv_hbm.1, f32[16,128]{1,0:T(8,128)} %bitcast.1), custom_call_target="tpu_custom_call" | custom-call | flops 1610612736 | bytes 4194304 | tf_op jit(solution)/shard_map/pallas_call | solution.py:248
  29.4 1.0 %copy.5 = bf16[256,2048]{1,0:T(8,128)(2,1)} copy(bf16[256,2048]{1,0:T(8,128)(2,1)S(1)} %shard_map.37) | data formatting | bytes 2097152

commit v4 on v3

--- a/solution.py
+++ b/solution.py
@@ -113,11 +113,10 @@
         >= lax.broadcasted_iota(jnp.int32, (group, BLK, BLK), 2)
     ).reshape(rows, BLK)
 
-    def step(h, b, slot, lo, nk, first=False, full=-1):
+    def scored(h, b, slot, lo, nk, first=False, full=-1):
         idx = h * 2 + b
         q = qbuf[pl.ds(h * group, group), b * BLK : (b + 1) * BLK, :].reshape(rows, HD)
         k = kvbuf[slot, h, 0, lo : lo + nk, :]
-        v = kvbuf[slot, h, 1, lo : lo + nk, :]
         s = lax.dot_general(q, k, (((1,), (1,)), ((), ())), preferred_element_type=F32)
         parts = [s[:, i : i + BLK] for i in range(0, nk, BLK)]
         parts = [x if i == full else jnp.where(lower, x, -jnp.inf) for i, x in enumerate(parts)]
@@ -127,15 +126,23 @@
             old = mbuf[idx]
             top = jnp.maximum(old, top)
         w = jnp.concatenate([jnp.exp2((x - top) * c).astype(BF16) for x in parts], axis=1)
-        pv = jnp.dot(
-            w, jnp.concatenate([v, ones[:nk]], axis=1), preferred_element_type=F32
-        )
         mbuf[idx] = top
-        if first:
-            acc[idx] = pv
-        else:
-            alpha = jnp.exp2((old - top) * c)
-            acc[idx] = acc[idx] * jnp.concatenate([alpha, alpha], axis=1) + pv
+        alpha = None if first else jnp.exp2((old - top) * c)
+
+        def finish():
+            v = kvbuf[slot, h, 1, lo : lo + nk, :]
+            pv = jnp.dot(
+                w, jnp.concatenate([v, ones[:nk]], axis=1), preferred_element_type=F32
+            )
+            if first:
+                acc[idx] = pv
+            else:
+                acc[idx] = acc[idx] * jnp.concatenate([alpha, alpha], axis=1) + pv
+
+        return finish
+
+    def step(*args, **options):
+        scored(*args, **options)()
 
     for h in range(kvh * group):
         q_load(h).wait()
@@ -200,9 +207,10 @@
             @pl.when(p >= 2**k)
             def _():
                 arrived(k, h, 0)
+                finish = [scored(h, b, k + 1, b * BLK, BLK) for b in range(2)]
                 arrived(k, h, 1)
-                step(h, 0, k + 1, 0, BLK)
-                step(h, 1, k + 1, BLK, BLK)
+                for rest in finish:
+                    rest()
 
         for b in range(2):
             idx = h * 2 + b

time: 30.5 us -> 30 us (0.984)
  Pallas kernels: 29.4 us -> 28.8 us
    pallas_call x1, Pallas kernels: 29.4 us -> 28.8 us  [local(): pl.pallas_call(body, out_shape=jax.ShapeDtypeStruct(queries.shape, BF16),...]
where the time goes in v4:
time: 30 us; the launch traced here: 29.8 us
  Pallas kernels  28.8 us (96%)
  local copies, waits for them, and re-layouts  0.97 us (3%)
    pallas_call x1, Pallas kernels, local(): pl.pallas_call(body, out_shape=jax.ShapeDtypeStruct(queries.shape, BF16),...  28.8 us
    unnamed x1, local copies, waits for them, and re-layouts  0.97 us

profile of v4, /device:TPU:17, one launch (start us, length us, event | category | flops | bytes accessed | tf_op | source)
XLA Modules:
  0.0 29.8 jit_solution(614238560253364507)
XLA Ops:
  0.0 28.8 %shard_map.37 = bf16[256,2048]{1,0:T(8,128)(2,1)S(1)} custom-call(bf16[256,2048]{1,0:T(8,128)(2,1)} %q_hbm.1, bf16[2,256,512]{2,1,0:T(8,128)(2,1)} %kv_hbm.1, f32[16,128]{1,0:T(8,128)} %bitcast.1), custom_call_target="tpu_custom_call" | custom-call | flops 1610612736 | bytes 4194304 | tf_op jit(solution)/shard_map/pallas_call | solution.py:256
  28.8 1.0 %copy.5 = bf16[256,2048]{1,0:T(8,128)(2,1)} copy(bf16[256,2048]{1,0:T(8,128)(2,1)S(1)} %shard_map.37) | data formatting | bytes 2097152
